TPU v7x, 512 devices: a whole 4x4x16 slice. The times are simulated.
512 devices in a mesh: lat: 32 (over z, core), wid: 16 (over x, y).
Axes of the slice: x: 4, y: 4, z: 16, core: 2. Of those that a mesh axis runs over, the one named last changes fastest.
Arguments:
- model_acts: bfloat16 [512, 4608], P(None, 'wid'), may hold values from -6 to 6
- picks: int32 [512, 64], replicated, may hold values from -1 to 32767, as said below
- group_ends: int32 [4], replicated, may hold values from 1 to 32768, as said below
- enc_weight: bfloat16 [4608, 32768], P('wid', 'lat'), may hold values from -0.09375 to 0.09375
- enc_bias: float32 [32768], P('lat'), may hold values from -3 to 3
- dec_weight: bfloat16 [32768, 4608], P('lat', 'wid'), may hold values from -1.5 to 1.5
- dec_bias: float32 [4608], P('wid'), may hold values from -3 to 3
Outputs:
- group_loss: float32 [512, 4], replicated
Inputs may be any that keep to these rules, and one draw needn't show every extreme that they name: `picks`: the ids of one row are distinct; the filled slots of a row come first, then -1; every row has between 16 and 64 filled slots, and some row has all 64. `group_ends`: strictly increasing; the last equals 32768.
All inputs are finite; a program needn't handle non-finite values.
Results may differ from a plain program's by a relative error of at most 0.007.
Values may be sent and summed in bfloat16 or wider, within the bound.
A program may use at most 128 MiB of HBM per device.

v0:
```python
import jax
import jax.numpy as jnp
from jax import lax
from jax.sharding import PartitionSpec as P


def prefix_2(x, axis, join, neutral):
    place = lax.axis_index(axis)
    gathered = lax.all_gather(x.astype(jnp.bfloat16), axis)
    state = jnp.zeros_like(x) + jnp.asarray(neutral, x.dtype)

    def one(step, state):
        return join(state, lax.dynamic_index_in_dim(gathered, step, 0, False).astype(x.dtype))

    return lax.fori_loop(0, place, one, state)


def fire(preact, pick_rows, enc_bias, first_latent):
    lat_dev = preact.shape[1]
    latent_ids = jnp.arange(lat_dev, dtype=jnp.int32)
    local_ids = pick_rows - first_latent
    slot_count = pick_rows.shape[1]
    stride = min(8, slot_count)
    hit = jnp.zeros(preact.shape, jnp.bool_)
    for begin in range(0, slot_count, stride):
        block_ids = local_ids[:, begin : begin + stride]
        hit = hit | jnp.any(block_ids[:, :, None] == latent_ids[None, None, :], axis=1)
    return jnp.where(hit, jax.nn.relu(preact + enc_bias), 0.0).astype(jnp.bfloat16)


def body(model_acts, picks, group_ends, enc_weight, enc_bias, dec_weight, dec_bias):
    row_count, shard_width = model_acts.shape
    lat_dev = enc_weight.shape[1]
    lat_index = lax.axis_index("lat")
    first_latent = lat_index * lat_dev
    centered = model_acts.astype(jnp.float32) - dec_bias
    enc_in = centered.astype(jnp.bfloat16)
    partial_sums = jnp.dot(enc_in, enc_weight, preferred_element_type=jnp.float32)
    preact = lax.psum(partial_sums.astype(jnp.bfloat16), "wid").astype(jnp.float32)
    acts = fire(preact, picks, enc_bias, first_latent)
    block_total = jnp.dot(acts, dec_weight, preferred_element_type=jnp.float32)
    carry_in = prefix_2(
        block_total, "lat", lambda earlier, later: earlier + later, jnp.zeros_like(block_total)
    )
    base_resid = centered - carry_in
    latent_ids = jnp.arange(lat_dev, dtype=jnp.int32)
    partials = []
    for group in range(group_ends.shape[0]):
        group_end = group_ends[group]
        local_limit = jnp.clip(group_end - first_latent, 0, lat_dev)
        kept_acts = jnp.where(latent_ids[None, :] < local_limit, acts, jnp.zeros_like(acts))
        prefix = jnp.dot(kept_acts, dec_weight, preferred_element_type=jnp.float32)
        owner_flag = ((group_end - 1) // lat_dev == lat_index).astype(jnp.float32)
        residual = base_resid - prefix
        partials.append(jnp.sum(residual * residual, axis=1) * owner_flag)
    squares = lax.psum(jnp.stack(partials, axis=1), ("lat", "wid"))
    return squares / (shard_width * lax.axis_size("wid"))


def solution(mesh):
    placed = (P(None, "wid"), P(), P(), P("wid", "lat"), P("lat"), P("lat", "wid"), P("wid"))
    return jax.shard_map(body, mesh=mesh, in_specs=placed, out_specs=P(), check_vma=False)
```

profile of v0, /device:TPU:1, one launch (start us, length us, event | category | flops | bytes accessed | tf_op | source)
XLA Modules:
  0.0 387.2 jit_solution(14715805781770319889)
XLA Ops:
  6.5 1.1 copy-done
  7.6 2.8 convolution_convert_fusion
  10.5 0.9 broadcast_subtract_fusion
  11.8 0.9 copy.21
  12.7 0.8 copy.22
  13.5 0.8 copy.23
  14.5 0.8 copy.25
  15.4 10.9 %fusion = (pred[512,1024]{1,0:T(8,128)(4,1)S(1)}, pred[512,1024]{1,0:T(8,128)(4,1)S(1)}) fusion(s32[512,8]{1,0:T(8,128)S(1)} %copy.18, s32[512,8]{1,0:T(8,128)S(1)} %copy.19), kind=kLoop, calls=%fused_computation.9 | loop fusion | flops 15728640 | bytes 1081344 | tf_op jit(solution)/shard_map/reduce_or | solution.py:27
  26.3 11.8 %fusion.2 = (pred[512,1024]{1,0:T(8,128)(4,1)S(1)}, pred[512,1024]{1,0:T(8,128)(4,1)S(1)}) fusion(s32[512,8]{1,0:T(8,128)S(1)} %copy.20, s32[512,8]{1,0:T(8,128)} %copy.21), kind=kLoop, calls=%fused_computation.11 | loop fusion | flops 15728640 | bytes 1081344 | tf_op jit(solution)/shard_map/reduce_or | solution.py:27
  38.1 12.7 %fusion.4 = (pred[512,1024]{1,0:T(8,128)(4,1)S(1)}, pred[512,1024]{1,0:T(8,128)(4,1)}) fusion(s32[512,8]{1,0:T(8,128)} %copy.22, s32[512,8]{1,0:T(8,128)} %copy.23), kind=kLoop, calls=%fused_computation.13 | loop fusion | flops 15728640 | bytes 1081344 | tf_op jit(solution)/shard_map/reduce_or | solution.py:27
  50.8 12.6 %fusion.6 = (pred[512,1024]{1,0:T(8,128)(4,1)}, pred[512,1024]{1,0:T(8,128)(4,1)}) fusion(s32[512,8]{1,0:T(8,128)S(1)} %copy.24, s32[512,8]{1,0:T(8,128)} %copy.25), kind=kLoop, calls=%fused_computation.15 | loop fusion | flops 15728640 | bytes 1081344 | tf_op jit(solution)/shard_map/reduce_or | solution.py:27
  63.4 68.9 %all-reduce.2.cloned.1.call-done = bf16[512,1024]{1,0:T(8,128)(2,1)} async-done(((bf16[512,1024]{1,0:T(8,128)(2,1)}), bf16[512,1024]{1,0:T(8,128)(2,1)}) %all-reduce.2.cloned.1.call-update) | async-done | bytes 1048592 | tf_op jit(solution)/shard_map/psum | solution.py:39
  132.3 3.1 select_convert_fusion
  135.4 1.0 copy-done.1
  136.4 2.3 convolution_convert_fusion.1
  144.5 76.1 %all-gather.3.cloned.1.call-done = bf16[16384,288]{0,1:T(8,128)(2,1)} async-done(((bf16[512,288]{0,1:T(8,128)(2,1)}), bf16[16384,288]{0,1:T(8,128)(2,1)}) %all-gather.3.cloned.1.call-update) | async-done | bytes 9437200 | tf_op jit(solution)/shard_map/all_gather | solution.py:9
  220.6 14.5 %copy.28 = bf16[16384,288]{1,0:T(8,128)(2,1)} copy(bf16[16384,288]{0,1:T(8,128)(2,1)} %all-gather.3.cloned.1.call-done) | data formatting | bytes 18874368 | tf_op jit(solution)/shard_map/while | solution.py:15
  235.1 1.2 while.10
  235.2 1.2 convert_add_fusion.2
  236.6 1.6 fusion.12
  238.2 1.6 fusion.13
  239.8 1.6 fusion.14
  241.4 1.6 fusion.15
  243.1 136.6 %psum.15 = f32[512,4]{0,1:T(4,128)S(1)} all-reduce(f32[512,4]{0,1:T(4,128)S(1)} %pad_maximum_fusion), channel_id=1, replica_groups=mesh['lat'=32,'wid'=16] {'lat','wid'}, use_global_device_ids=true, to_apply=%region_15.16 | all-reduce | flops 2048 | bytes 16384 | tf_op jit(solution)/shard_map/psum | solution.py:56
  (32 shorter events, 2.2 us)
Async XLA Ops:
  6.5 1.1 copy-start
  6.5 132.1 %copy-start.3 = (s32[4]{0:T(128)S(1)}, s32[4]{0:T(128)}, u32[]{:S(2)}) copy-start(s32[4]{0:T(128)} %param.11) | copy-start | bytes 52
  6.5 125.8 %all-reduce.2.cloned.1.call-start = ((), (), s32[]{:S(2)}) async-start(), calls=%async_computation | async-start | bytes 2097152 | tf_op jit(solution)/shard_map/psum | solution.py:39
  10.4 210.2 %all-gather.3.cloned.1.call-start = ((), (), s32[]{:S(2)}) async-start(), calls=%async_computation.1 | async-start | bytes 9732096 | tf_op jit(solution)/shard_map/all_gather | solution.py:9
  135.4 1.0 copy-start.1
  144.5 92.1 %copy-start.2 = (bf16[512,1024]{1,0:T(8,128)(2,1)S(1)}, bf16[512,1024]{1,0:T(8,128)(2,1)}, u32[]{:S(2)}) copy-start(bf16[512,1024]{1,0:T(8,128)(2,1)} %copy-done.1) | copy-start | bytes 3145732
  144.5 92.1 %copy-start.4 = (bf16[512,288]{0,1:T(8,128)(2,1)S(1)}, bf16[512,288]{0,1:T(8,128)(2,1)}, u32[]{:S(2)}) copy-start(bf16[512,288]{0,1:T(8,128)(2,1)} %param.9) | copy-start | bytes 884740
  144.5 92.1 %copy-start.5 = (f32[288]{0:T(512)S(1)}, f32[288]{0:T(512)}, u32[]{:S(2)}) copy-start(f32[288]{0:T(512)} %param.15) | copy-start | bytes 3460
Sparse Core Ops, SparseCore 0:
  10.6 121.6 all-reduce.1
  138.8 81.7 all-gather.2
where the time goes:
time: 389 us; the launch traced here: 387 us
  waiting for transfers between devices  145 us (37%)
  blocking collectives  137 us (35%)
  other arithmetic  53.8 us (14%)
  local copies, waits for them, and re-layouts  21.4 us (6%)
  between operations  18.7 us (5%)
  matrix products  11.5 us (3%)
    psum x1, blocking collectives, body(): squares = lax.psum(jnp.stack(partials, axis=1), ('lat', 'wid'))  137 us
    all_gather x1, waiting for transfers between devices, prefix_2(): gathered = lax.all_gather(x.astype(jnp.bfloat16), axis)  76.1 us
    psum x1, waiting for transfers between devices, body(): lax.psum(partial_sums.astype(jnp.bfloat16), 'wid').astype(jnp.float32)  68.9 us
    reduce_or x4, other arithmetic, fire(): jnp.any(block_ids[:, :, None] == latent_ids[None, None, :], axis=1)  48 us
    while x2, local copies, waits for them, and re-layouts, prefix_2(): return lax.fori_loop(0, place, one, state)  14.7 us
  transfers between devices with their start and end apart: 2, of which 2 were waited for; matrix products, arithmetic and copies ran while one was open for 14% of the time, Pallas kernels for 0%

commit v1 on v0

v1 whole, which is shorter than its diff:
```python
import jax
import jax.numpy as jnp
from jax import lax
from jax.experimental import pallas as pl
from jax.experimental.pallas import tpu as pltpu
from jax.sharding import PartitionSpec as P

F32, BF16, I32 = jnp.float32, jnp.bfloat16, jnp.int32
ROWS, KMAX, GROUPS = 512, 64, 4
SHARD, MAIN = 288, 256
REM = SHARD - MAIN
LAT_DEV = 1024
N_LAT, N_WID, N_Z = 32, 16, 16
CHUNK = 16
WIDE = GROUPS * SHARD

LEVEL_1 = (
    (5, 1), (7, -1), (-7, 1), (-5, -1), (8, -2),
    (2, 1), (4, -1), (-4, 1), (-2, -1),
    (1, -1), (-1, 1),
)
CENTRES = (6, -6, 3, -3)
Z_PEERS = (1, -1, 2, -2, 3, -3, 6, -6)


def members(centre):
    return [k for k, (offset, dz) in enumerate(LEVEL_1) if offset + dz == centre]


def kernel(
    x_hbm, picks_hbm, ends_ref, encw_hbm, encb_hbm, dec_hbm, decb_hbm, out_ref,
    x_v, picks_v, encw_v, encb_v, dec_v, decb_v,
    xs, part, ids, lo_s, w0_s, w1_s, u0_t, u1_t, u0, u1, masked_dec,
    a1_src, a1_slot, acts_c, dens, to_sib, own, from_sib,
    l1_src, l1_slot, l2_src, l2_slot, c1_src, c1_slot, c2_src, c2_slot,
    in_sem, a1_send, a1_recv, a2_send, a2_recv, sib_send, sib_recv,
    l1_send, l1_recv, l2_send, l2_recv, c1_send, c1_recv, c2_send, c2_recv,
):
    lat = lax.axis_index("lat")
    wid = lax.axis_index("wid")
    z, core = lat // 2, lat % 2
    first = lat * LAT_DEV

    def in_plane(step):
        return (lat, lax.rem(wid + step, N_WID))

    def along_z(step):
        return (lax.rem(z + step + N_Z, N_Z) * 2 + core, wid)

    sibling = (lat + 1 - 2 * core, wid)

    def send(src, dst, s_sem, r_sem, device):
        return pltpu.make_async_remote_copy(
            src_ref=src, dst_ref=dst, send_sem=s_sem, recv_sem=r_sem,
            device_id=device, device_id_type=pl.DeviceIdType.MESH,
        )

    loads = [
        pltpu.make_async_copy(src, dst, in_sem.at[i])
        for i, (src, dst) in enumerate(
            ((x_hbm, x_v), (encw_hbm, encw_v), (decb_hbm, decb_v), (picks_hbm, picks_v),
             (encb_hbm, encb_v), (dec_hbm, dec_v))
        )
    ]
    for load in loads:
        load.start()

    barrier = pltpu.get_barrier_semaphore()

    def greet(device):
        pl.semaphore_signal(barrier, inc=1, device_id=device, device_id_type=pl.DeviceIdType.MESH)

    for step in Z_PEERS:
        greet(along_z(step))
    for step in range(1, N_WID):
        greet(in_plane(step))
    greet(sibling)

    loads[0].wait()
    loads[1].wait()
    loads[2].wait()
    x_t = x_v[...].astype(F32)
    tail = x_t[MAIN:, :]
    lanes_1 = lax.broadcasted_iota(I32, (1, 128), 1)
    bias_tail = jnp.concatenate([decb_v[:, MAIN:], jnp.zeros((1, 128 - REM), F32)], axis=1)
    bias_tail = jnp.where(lanes_1 < REM, bias_tail, 0.0)
    bias_tail = jnp.broadcast_to(bias_tail, (8, 128))
    bias_tail = (bias_tail + pltpu.roll(bias_tail, REM, 1)) + (
        pltpu.roll(bias_tail, 2 * REM, 1) + pltpu.roll(bias_tail, 3 * REM, 1))
    bias = jnp.concatenate([decb_v[:, :MAIN], bias_tail[:1, :]], axis=1)
    xs[...] = jnp.concatenate([x_t, tail, tail, tail], axis=0).T - bias
    part[...] = jnp.dot(
        xs[:, :SHARD].astype(BF16), encw_v[...], preferred_element_type=F32
    )

    loads[3].wait()
    loads[4].wait()
    local = picks_v[...] - first
    ids[...] = jnp.concatenate([local[:, :ROWS // 2], local[:, ROWS // 2:]], axis=0).T

    def picked(row):
        halves = []
        for sub in range(2):
            r = pl.multiple_of(row + 8 * sub, 8)
            r_2 = pl.multiple_of(row + 8 * sub + ROWS // 2, 8)
            where = ids[pl.ds(r, 8), :]
            lo, hi = where & 127, where >> 7
            lane = lax.broadcasted_iota(I32, (8, 128), 1)
            got = jnp.zeros((8, 128), F32)
            for h in range(8):
                cols = slice(128 * h, 128 * h + 128)
                here = jnp.where(
                    lane < KMAX,
                    jnp.take_along_axis(part[pl.ds(r, 8), cols], lo, 1, mode="promise_in_bounds"),
                    jnp.take_along_axis(part[pl.ds(r_2, 8), cols], lo, 1, mode="promise_in_bounds"),
                )
                got = jnp.where(hi == h, here, got)
            halves.append(got)
        return jnp.concatenate(halves, axis=0).astype(BF16)

    pl.semaphore_wait(barrier, len(Z_PEERS) + N_WID)

    def a1_copy(step):
        target = lax.rem(wid + step, N_WID)
        return send(a1_src.at[target], a1_slot.at[wid], a1_send.at[step], a1_recv.at[step], (lat, target))

    def a1_step(step, carry):
        target = lax.rem(wid + step, N_WID)
        a1_src[target] = picked(target * CHUNK)
        a1_copy(step).start()
        return carry

    lax.fori_loop(1, N_WID, a1_step, 0)
    my_rows = pl.multiple_of(wid * CHUNK, CHUNK)
    a1_slot[wid] = picked(my_rows)

    mine = ids[pl.ds(my_rows, CHUNK), :]
    hit = (mine >= 0) & (mine < LAT_DEV)
    my_bias = jnp.zeros((CHUNK, 128), F32)
    for h in range(8):
        row = jnp.broadcast_to(encb_v[:, 128 * h:128 * h + 128], (CHUNK, 128))
        my_bias = jnp.where(
            mine >> 7 == h, jnp.take_along_axis(row, mine & 127, 1, mode="promise_in_bounds"), my_bias)

    high = local >> 7
    inside = (local >= 0) & (local < LAT_DEV)
    field = (lax.broadcasted_iota(I32, local.shape, 0) + 1) << ((high & 3) * 8)
    lo_s[...] = local & 127
    w0_s[...] = jnp.where(inside & (high < 4), field, 0)
    w1_s[...] = jnp.where(inside & (high >= 4), field, 0)

    def fields(it, carry):
        cols = pl.ds(pl.multiple_of((it // 4) * 128, 128), 128)
        low = pl.multiple_of((it % 4) * 32, 32)
        iota = lax.broadcasted_iota(I32, (32, 128), 0) + low

        def eight(k8, acc):
            acc_0, acc_1 = acc
            rows = pl.ds(pl.multiple_of(k8 * 8, 8), 8)
            lo_8, w0_8, w1_8 = lo_s[rows, cols], w0_s[rows, cols], w1_s[rows, cols]
            for k in range(8):
                same = jnp.broadcast_to(lo_8[k:k + 1, :], (32, 128)) == iota
                acc_0 = acc_0 | jnp.where(same, jnp.broadcast_to(w0_8[k:k + 1, :], (32, 128)), 0)
                acc_1 = acc_1 | jnp.where(same, jnp.broadcast_to(w1_8[k:k + 1, :], (32, 128)), 0)
            return acc_0, acc_1

        zero = jnp.zeros((32, 128), I32)
        acc_0, acc_1 = lax.fori_loop(0, KMAX // 8, eight, (zero, zero))
        u0_t[pl.ds(low, 32), cols] = acc_0
        u1_t[pl.ds(low, 32), cols] = acc_1
        return carry

    lax.fori_loop(0, 16, fields, 0)
    u0[...] = u0_t[...].T
    u1[...] = u1_t[...].T

    for step in range(1, N_WID):
        a1_copy(step).wait_recv()
    total = jnp.zeros((CHUNK, 128), F32)
    for w in range(N_WID):
        total = total + a1_slot[w].astype(F32)
    acts_c[pl.ds(my_rows, CHUNK), :] = jnp.where(
        hit, jnp.maximum(total + my_bias, 0.0), 0.0).astype(BF16)

    def a2_copy(step):
        rows = acts_c.at[pl.ds(my_rows, CHUNK), :]
        return send(rows, rows, a2_send.at[step], a2_recv.at[step], in_plane(step))

    for step in range(1, N_WID):
        a2_copy(step).start()

    loads[5].wait()
    latent = lax.broadcasted_iota(I32, (1, LAT_DEV), 1) + first
    for g in range(GROUPS):
        keep = jnp.where(latent < ends_ref[g], 1.0, 0.0).astype(BF16)
        masked_dec[MAIN * g:MAIN * g + MAIN, :] = dec_v[:MAIN, :] * keep
        at = GROUPS * MAIN + REM * g
        masked_dec[at:at + REM, :] = dec_v[MAIN:, :] * keep

    for step in range(1, N_WID):
        a2_copy(step).wait_recv()

    lane_16 = lax.broadcasted_iota(I32, (16, 128), 1)

    def densify(half):
        def one(i, carry):
            r_c = pl.multiple_of(i * 16, 16)
            r = pl.multiple_of(half * (ROWS // 2) + i * 16, 16)
            values = pltpu.roll(acts_c[pl.ds(r_c, 16), :].astype(F32), 1 + KMAX * half, 1)
            values = jnp.where((lane_16 >= 1) & (lane_16 <= KMAX), values, 0.0)
            words = (u0[pl.ds(r, 16), :], u1[pl.ds(r, 16), :])
            for h in range(8):
                slot = (words[h // 4] >> (8 * (h % 4))) & 127
                dens[pl.ds(r, 16), 128 * h:128 * h + 128] = jnp.take_along_axis(
                    values, slot, 1, mode="promise_in_bounds").astype(BF16)
            return carry

        lax.fori_loop(0, ROWS // 32, one, 0)

    def decode(half):
        rows = pl.ds(pl.multiple_of(half * (ROWS // 2), ROWS // 2), ROWS // 2)
        return lax.dot_general(
            dens[rows, :], masked_dec[...], (((1,), (1,)), ((), ())), preferred_element_type=F32
        ).astype(BF16)

    def sib_copy(i):
        rows = pl.ds(64 * i, 64)
        return send(to_sib.at[rows], from_sib.at[rows], sib_send.at[i], sib_recv.at[i], sibling)

    densify(1 - core)
    to_sib[...] = decode(1 - core)
    for i in range(4):
        sib_copy(i).start()
    densify(core)
    own[...] = decode(core)
    for i in range(4):
        sib_copy(i).wait_recv()

    def chip_sum(offset):
        p = lax.rem(z - offset + N_Z, N_Z)
        rows = pl.ds(pl.multiple_of(p * CHUNK, CHUNK), CHUNK)
        return own[rows, :].astype(F32) + from_sib[rows, :].astype(F32)

    def l1_copy(k):
        return send(l1_src.at[k], l1_slot.at[k], l1_send.at[k], l1_recv.at[k], along_z(LEVEL_1[k][1]))

    def l2_copy(j):
        return send(l2_src.at[j], l2_slot.at[j], l2_send.at[j], l2_recv.at[j], along_z(-CENTRES[j]))

    for k, (offset, _) in enumerate(LEVEL_1):
        l1_src[k] = chip_sum(offset).astype(BF16)
        l1_copy(k).start()
    for j, centre in enumerate(CENTRES):
        acc = chip_sum(centre)
        for k in members(centre):
            l1_copy(k).wait_recv()
            acc = acc + l1_slot[k].astype(F32)
        l2_src[j] = acc.astype(BF16)
        l2_copy(j).start()
    prefix = chip_sum(0)
    for k in members(0):
        l1_copy(k).wait_recv()
        prefix = prefix + l1_slot[k].astype(F32)
    for j in (2, 3, 0, 1):
        l2_copy(j).wait_recv()
        prefix = prefix + l2_slot[j].astype(F32)

    row_0 = core * (ROWS // 2) + z * CHUNK
    centered = xs[pl.ds(pl.multiple_of(row_0, CHUNK), CHUNK), :]
    err_tail = centered[:, MAIN:] - prefix[:, GROUPS * MAIN:]
    sq_tail = err_tail * err_tail
    row_16 = lax.broadcasted_iota(I32, (16, 128), 0)
    placed = jnp.zeros((16, 128), F32)
    for g in range(GROUPS):
        err = centered[:, :MAIN] - prefix[:, MAIN * g:MAIN * g + MAIN]
        sq = err * err
        sq = sq[:, :128] + sq[:, 128:] + jnp.where(lane_16 // REM == g, sq_tail, 0.0)
        loss = jnp.sum(sq, axis=1, keepdims=True)
        placed = placed + jnp.where(lane_16 == lax.rem(z + g, 8) * 16 + row_16, loss, 0.0)
    partial = jnp.sum(placed, axis=0, keepdims=True)

    def c1_copy(step):
        return send(c1_src, c1_slot.at[wid], c1_send.at[step], c1_recv.at[step], in_plane(step))

    c1_src[...] = partial
    for step in range(1, N_WID):
        c1_copy(step).start()
    c1_slot[wid] = partial
    for step in range(1, N_WID):
        c1_copy(step).wait_recv()
    total_loss = c1_slot[0]
    for w in range(1, N_WID):
        total_loss = total_loss + c1_slot[w]
    total_loss = total_loss / (SHARD * N_WID)

    place = core * N_Z + z

    def c2_copy(step):
        return send(c2_src, c2_slot.at[place], c2_send.at[step], c2_recv.at[step],
                    (lax.rem(lat + step, N_LAT), wid))

    c2_src[...] = total_loss
    for step in range(1, N_LAT):
        c2_copy(step).start()
    c2_slot[place] = total_loss

    for step in range(1, N_WID):
        a1_copy(step).wait_send()
        a2_copy(step).wait_send()
        c1_copy(step).wait_send()
    for i in range(4):
        sib_copy(i).wait_send()
    for k in range(len(LEVEL_1)):
        l1_copy(k).wait_send()
    for j in range(len(CENTRES)):
        l2_copy(j).wait_send()
    for step in range(1, N_LAT):
        c2_copy(step).wait_recv()

    lane_8 = lax.broadcasted_iota(I32, (8, 128), 1)
    sub_8 = lax.broadcasted_iota(I32, (8, 128), 0)
    for b in range(ROWS // 128):
        block = jnp.concatenate([c2_slot[8 * b + m] for m in range(8)], axis=0)
        for g in range(GROUPS):
            line = jnp.sum(jnp.where(lane_8 // 16 == (sub_8 + g) % 8, block, 0.0), axis=0, keepdims=True)
            line = jnp.broadcast_to(line, (8, 128))
            if g:
                line = pltpu.roll(line, 128 - 16 * g, 1)
            out_ref[g:g + 1, 128 * b:128 * b + 128] = line[:1, :]
    for step in range(1, N_LAT):
        c2_copy(step).wait_send()


def body(model_acts, picks, group_ends, enc_weight, enc_bias, dec_weight, dec_bias):
    vmem, dma = pltpu.VMEM, pltpu.SemaphoreType.DMA
    half = ROWS // 2
    n_1, n_2 = len(LEVEL_1), len(CENTRES)
    anywhere = pl.BlockSpec(memory_space=pl.ANY)
    losses = pl.pallas_call(
        kernel,
        out_shape=jax.ShapeDtypeStruct((GROUPS, ROWS), F32),
        in_specs=[anywhere, anywhere, pl.BlockSpec(memory_space=pltpu.SMEM)] + [anywhere] * 4,
        out_specs=pl.BlockSpec(memory_space=pltpu.VMEM),
        scratch_shapes=[
            vmem((SHARD, ROWS), BF16), vmem((KMAX, ROWS), I32), vmem((SHARD, LAT_DEV), BF16),
            vmem((1, LAT_DEV), F32), vmem((SHARD, LAT_DEV), BF16), vmem((1, SHARD), F32),
            vmem((ROWS, MAIN + 128), F32), vmem((ROWS, LAT_DEV), F32), vmem((half, 128), I32),
            vmem((KMAX, ROWS), I32), vmem((KMAX, ROWS), I32), vmem((KMAX, ROWS), I32),
            vmem((128, ROWS), I32), vmem((128, ROWS), I32), vmem((ROWS, 128), I32), vmem((ROWS, 128), I32),
            vmem((WIDE, LAT_DEV), BF16),
            vmem((N_WID, CHUNK, 128), BF16), vmem((N_WID, CHUNK, 128), BF16), vmem((half, 128), BF16),
            vmem((ROWS, LAT_DEV), BF16), vmem((half, WIDE), BF16), vmem((half, WIDE), BF16),
            vmem((half, WIDE), BF16),
            vmem((n_1, CHUNK, WIDE), BF16), vmem((n_1, CHUNK, WIDE), BF16),
            vmem((n_2, CHUNK, WIDE), BF16), vmem((n_2, CHUNK, WIDE), BF16),
            vmem((1, 128), F32), vmem((N_WID, 1, 128), F32), vmem((1, 128), F32), vmem((N_LAT, 1, 128), F32),
            dma((6,)), dma((N_WID,)), dma((N_WID,)), dma((N_WID,)), dma((N_WID,)), dma((4,)), dma((4,)),
            dma((n_1,)), dma((n_1,)), dma((n_2,)), dma((n_2,)),
            dma((N_WID,)), dma((N_WID,)), dma((N_LAT,)), dma((N_LAT,)),
        ],
        compiler_params=pltpu.CompilerParams(
            collective_id=0, has_side_effects=True, vmem_limit_bytes=48 * 2 ** 20),
    )(
        model_acts.T, picks.T, group_ends, enc_weight, enc_bias.reshape(1, -1), dec_weight.T,
        dec_bias.reshape(1, -1),
    )
    return losses.T


def solution(mesh):
    placed = (P(None, "wid"), P(), P(), P("wid", "lat"), P("lat"), P("lat", "wid"), P("wid"))
    return jax.shard_map(body, mesh=mesh, in_specs=placed, out_specs=P(), check_vma=False)
```

time: 389 us -> 71.5 us (0.18)
  waiting for transfers between devices: 145 us -> 0 us
  blocking collectives: 137 us -> 0 us
  Pallas kernels: 0 us -> 65.3 us
  other arithmetic: 53.8 us -> 0 us
  between operations: 18.7 us -> 0.02 us
  local copies, waits for them, and re-layouts: 21.4 us -> 5.93 us
  matrix products: 11.5 us -> 0 us
    psum x1 -> x0, blocking collectives: 137 us -> none  [body(): squares = lax.psum(jnp.stack(partials, axis=1), ('lat', 'wid'))]
    all_gather x1 -> x0, waiting for transfers between devices: 76.1 us -> none  [prefix_2(): gathered = lax.all_gather(x.astype(jnp.bfloat16), axis)]
    psum x1 -> x0, waiting for transfers between devices: 68.9 us -> none  [body(): lax.psum(partial_sums.astype(jnp.bfloat16), 'wid').astype(jnp.float32)]
    pallas_call x0 -> x1, Pallas kernels: none -> 65.3 us  [body(): pl.pallas_call(kernel, out_shape=jax.ShapeDtypeStruct((GROUPS, ROWS), F32...]
    reduce_or x4 -> x0, other arithmetic: 48 us -> none  [fire(): jnp.any(block_ids[:, :, None] == latent_ids[None, None, :], axis=1)]
    while x2 -> x0, local copies, waits for them, and re-layouts: 14.7 us -> none  [prefix_2(): return lax.fori_loop(0, place, one, state)]
    dot_general x6 -> x0, matrix products: 11.5 us -> none  [the longest x4 6.45 us: body(): prefix = jnp.dot(kept_acts, dec_weight, preferred_element_type=jnp.float32)]
    slice x10 -> x0, local copies, waits for them, and re-layouts: 4.56 us -> none  [the longest x9 3.89 us: fire(): block_ids = local_ids[:, begin:begin + stride]]
  transfers between devices with their start and end apart: 2 -> 0, of which waited for: 2 -> 0; matrix products, arithmetic and copies ran while one was open for 14% -> 0% of each run, Pallas kernels for 0% -> 0%
where the time goes in v1:
time: 71.5 us; the launch traced here: 71.2 us
  Pallas kernels  65.3 us (91%)
  local copies, waits for them, and re-layouts  5.93 us (8%)
    pallas_call x1, Pallas kernels, body(): pl.pallas_call(kernel, out_shape=jax.ShapeDtypeStruct((GROUPS, ROWS), F32...  65.3 us
    unnamed x15, local copies, waits for them, and re-layouts  5.93 us

profile of v1, /device:TPU:1, one launch (start us, length us, event | category | flops | bytes accessed | tf_op | source)
XLA Modules:
  0.0 71.2 jit_solution(1616006033789498243)
XLA Ops:
  0.0 0.0 copy-start.6
  0.0 0.0 copy-start.4
  0.0 0.7 copy-done.6
  0.7 0.0 copy-start.5
  0.7 0.0 copy-done.4
  0.7 0.6 copy-done.5
  1.3 0.0 copy-start
  1.3 1.1 %copy-done = bf16[288,1024]{1,0:T(8,128)(2,1)S(1)} copy-done((bf16[288,1024]{1,0:T(8,128)(2,1)S(1)}, bf16[288,1024]{1,0:T(8,128)(2,1)}, u32[]{:S(2)}) %copy-start) | copy-done | bytes 589848
  2.4 0.0 copy-start.1
  2.4 1.1 %copy-done.1 = bf16[1024,288]{0,1:T(8,128)(2,1)S(1)} copy-done((bf16[1024,288]{0,1:T(8,128)(2,1)S(1)}, bf16[1024,288]{0,1:T(8,128)(2,1)}, u32[]{:S(2)}) %copy-start.1) | copy-done | bytes 589848
  3.5 0.0 copy-start.2
  3.5 1.0 %copy-done.2 = bf16[512,288]{0,1:T(8,128)(2,1)S(1)} copy-done((bf16[512,288]{0,1:T(8,128)(2,1)S(1)}, bf16[512,288]{0,1:T(8,128)(2,1)}, u32[]{:S(2)}) %copy-start.2) | copy-done | bytes 294936
  4.4 0.0 copy-start.3
  4.4 0.9 %copy-done.3 = s32[512,64]{0,1:T(8,128)S(1)} copy-done((s32[512,64]{0,1:T(8,128)S(1)}, s32[512,64]{0,1:T(8,128)}, u32[]{:S(2)}) %copy-start.3) | copy-done | bytes 131096
  5.3 65.3 %shard_map.73 = f32[4,512]{1,0:T(4,128)S(1)} custom-call(bf16[288,512]{1,0:T(8,128)(2,1)S(1)} %bitcast.6, s32[64,512]{1,0:T(8,128)S(1)} %bitcast.7, s32[4]{0:T(128)S(1)} %copy-done.5, bf16[288,1024]{1,0:T(8,128)(2,1)S(1)} %copy-done, f32[1,1024]{1,0:T(1,128)S(1)} %bitcast.9, bf16[288,1024]{1,0:T(8,128)(2,1)S(1)} %bitcast.5, f32[1,288]{1,0:T(1,128)S(1)} %reshape.7.decb_hbm), custom_call_target="tpu_custom_call" | custom-call | tf_op jit(solution)/shard_map/pallas_call | solution.py:339
  70.6 0.6 copy.9
  (1 shorter events, 0.0 us)
Async XLA Ops:
  0.0 0.7 copy-start.6
  0.0 0.7 copy-start.4
  0.7 0.7 copy-start.5
  1.3 1.1 %copy-start = (bf16[288,1024]{1,0:T(8,128)(2,1)S(1)}, bf16[288,1024]{1,0:T(8,128)(2,1)}, u32[]{:S(2)}) copy-start(bf16[288,1024]{1,0:T(8,128)(2,1)} %encw_hbm.1) | copy-start | bytes 1769476
  2.4 1.1 %copy-start.1 = (bf16[1024,288]{0,1:T(8,128)(2,1)S(1)}, bf16[1024,288]{0,1:T(8,128)(2,1)}, u32[]{:S(2)}) copy-start(bf16[1024,288]{0,1:T(8,128)(2,1)} %param.12) | copy-start | bytes 1769476
  3.5 1.0 %copy-start.2 = (bf16[512,288]{0,1:T(8,128)(2,1)S(1)}, bf16[512,288]{0,1:T(8,128)(2,1)}, u32[]{:S(2)}) copy-start(bf16[512,288]{0,1:T(8,128)(2,1)} %param.7) | copy-start | bytes 884740
  4.4 0.9 %copy-start.3 = (s32[512,64]{0,1:T(8,128)S(1)}, s32[512,64]{0,1:T(8,128)}, u32[]{:S(2)}) copy-start(s32[512,64]{0,1:T(8,128)} %param.8) | copy-start | bytes 393220

commit v2 on v1

v2 whole, which is shorter than its diff:
```python
import jax
import jax.numpy as jnp
from jax import lax
from jax.experimental import pallas as pl
from jax.experimental.pallas import tpu as pltpu
from jax.sharding import PartitionSpec as P

F32, BF16, I32 = jnp.float32, jnp.bfloat16, jnp.int32
ROWS, KMAX, GROUPS = 512, 64, 4
SHARD, MAIN = 288, 256
REM = SHARD - MAIN
LAT_DEV = 1024
EXTRACT = 32
N_LAT, N_WID, N_Z = 32, 16, 16
CHUNK = 16
WIDE = GROUPS * SHARD

LEVEL_1 = (
    (5, 1), (7, -1), (-7, 1), (-5, -1), (8, -2),
    (2, 1), (4, -1), (-4, 1), (-2, -1),
    (1, -1), (-1, 1),
)
CENTRES = (6, -6, 3, -3)
Z_PEERS = (3, -3, 2, -2, 1, -1)


def ring(step, size):
    return min(step % size, -step % size)


PLANE = sorted(
    ((dx, dy) for dx in range(4) for dy in range(4) if dx or dy),
    key=lambda d: -(ring(d[0], 4) + ring(d[1], 4)))
COLUMN = sorted(
    ((dz, dc) for dz in range(N_Z) for dc in range(2) if dz or dc), key=lambda d: -ring(d[0], N_Z))
ARRIVALS = (range(14, 4, -1), range(4, -1, -1))


def members(centre):
    return [k for k, (offset, dz) in enumerate(LEVEL_1) if offset + dz == centre]


def kernel(
    x_hbm, picks_hbm, ends_ref, encw_hbm, encb_hbm, dec_hbm, decb_v, out_ref,
    x_v, picks_v, encw_v, encb_v, dec_v,
    xs, part, ids, lo_s, w0_s, w1_s, u0_t, u1_t, u0, u1, masked_dec,
    a1_src, a1_slot, acts_c, dens, to_sib, own, from_sib,
    l1_src, l1_slot, l2_src, l2_slot, c1_src, c1_slot, c2_src, c2_slot,
    in_sem, a1_send, a1_recv, a2_send, a2_recv, sib_send, sib_recv,
    far_ready, l1_send, l1_recv, l2_send, l2_recv, c1_send, c1_recv, c2_send, c2_recv,
):
    lat = lax.axis_index("lat")
    wid = lax.axis_index("wid")
    z, core = lat // 2, lat % 2
    first = lat * LAT_DEV

    def plane(j, sign=1):
        dx, dy = PLANE[j]
        return (wid // 4 + 4 + sign * dx) % 4 * 4 + (wid % 4 + 4 + sign * dy) % 4

    def in_plane(j):
        return (lat, plane(j))

    def along_z(step):
        return (lax.rem(z + step + N_Z, N_Z) * 2 + core, wid)

    sibling = (lat + 1 - 2 * core, wid)

    def send(src, dst, s_sem, r_sem, device):
        return pltpu.make_async_remote_copy(
            src_ref=src, dst_ref=dst, send_sem=s_sem, recv_sem=r_sem,
            device_id=device, device_id_type=pl.DeviceIdType.MESH,
        )

    loads = [
        pltpu.make_async_copy(src, dst, in_sem.at[i])
        for i, (src, dst) in enumerate(
            ((x_hbm, x_v), (encw_hbm, encw_v), (picks_hbm, picks_v),
             (encb_hbm, encb_v), (dec_hbm, dec_v))
        )
    ]
    barrier = pltpu.get_barrier_semaphore()

    def greet(device):
        pl.semaphore_signal(barrier, inc=1, device_id=device, device_id_type=pl.DeviceIdType.MESH)

    for step in Z_PEERS:
        greet(along_z(step))
    for j in range(len(PLANE)):
        greet(in_plane(j))
    greet(sibling)
    for load in loads:
        load.start()
    pending = []

    loads[0].wait()
    loads[1].wait()
    x_t = x_v[...].astype(F32)
    tail = x_t[MAIN:, :]
    lanes_1 = lax.broadcasted_iota(I32, (1, 128), 1)
    bias_tail = jnp.concatenate([decb_v[MAIN:].reshape(1, REM), jnp.zeros((1, 128 - REM), F32)], axis=1)
    bias_tail = jnp.where(lanes_1 < REM, bias_tail, 0.0)
    bias_tail = jnp.broadcast_to(bias_tail, (8, 128))
    bias_tail = (bias_tail + pltpu.roll(bias_tail, REM, 1)) + (
        pltpu.roll(bias_tail, 2 * REM, 1) + pltpu.roll(bias_tail, 3 * REM, 1))
    bias = jnp.concatenate([decb_v[:MAIN].reshape(1, MAIN), bias_tail[:1, :]], axis=1)
    xs[...] = jnp.concatenate([x_t, tail, tail, tail], axis=0).T - bias
    part[...] = jnp.dot(
        xs[:, :SHARD].astype(BF16), encw_v[...], preferred_element_type=F32
    )

    loads[2].wait()
    loads[3].wait()
    local = picks_v[...] - first
    ids[...] = jnp.concatenate([local[:, :ROWS // 2], local[:, ROWS // 2:]], axis=0).T

    lane_e = lax.broadcasted_iota(I32, (EXTRACT, 128), 1)

    def extract(i, carry):
        r = pl.multiple_of(i * EXTRACT, EXTRACT)
        r_2 = pl.multiple_of(i * EXTRACT + ROWS // 2, EXTRACT)
        where = ids[pl.ds(r, EXTRACT), :]
        lo, hi = where & 127, where >> 7
        got = jnp.zeros((EXTRACT, 128), F32)
        for h in range(8):
            cols = slice(128 * h, 128 * h + 128)
            here = jnp.where(
                lane_e < KMAX,
                jnp.take_along_axis(part[pl.ds(r, EXTRACT), cols], lo, 1, mode="promise_in_bounds"),
                jnp.take_along_axis(part[pl.ds(r_2, EXTRACT), cols], lo, 1, mode="promise_in_bounds"),
            )
            got = jnp.where(hi == h, here, got)
        a1_src[pl.ds(r, EXTRACT), :] = got.astype(BF16)
        return carry

    lax.fori_loop(0, ROWS // 2 // EXTRACT, extract, 0)

    pl.semaphore_wait(barrier, len(Z_PEERS) + N_WID)
    def a1_copy(j):
        target = plane(j)
        rows = pl.ds(pl.multiple_of(target * CHUNK, CHUNK), CHUNK)
        return send(a1_src.at[rows], a1_slot.at[wid], a1_send.at[j], a1_recv.at[j], (lat, target))

    for j in range(len(PLANE)):
        a1_copy(j).start()
        pending.append(a1_copy(j))
    for i, step in enumerate((3, -3)):
        pl.semaphore_signal(
            far_ready.at[i], inc=1, device_id=along_z(step), device_id_type=pl.DeviceIdType.MESH)
    my_rows = pl.multiple_of(wid * CHUNK, CHUNK)
    a1_slot[wid] = a1_src[pl.ds(my_rows, CHUNK), :]

    mine = ids[pl.ds(my_rows, CHUNK), :]
    hit = (mine >= 0) & (mine < LAT_DEV)
    my_bias = jnp.zeros((CHUNK, 128), F32)
    for h in range(8):
        row = jnp.broadcast_to(encb_v[:, 128 * h:128 * h + 128], (CHUNK, 128))
        my_bias = jnp.where(
            mine >> 7 == h, jnp.take_along_axis(row, mine & 127, 1, mode="promise_in_bounds"), my_bias)

    high = local >> 7
    inside = (local >= 0) & (local < LAT_DEV)
    field = (lax.broadcasted_iota(I32, local.shape, 0) + 1) << ((high & 3) * 8)
    lo_s[...] = local & 127
    w0_s[...] = jnp.where(inside & (high < 4), field, 0)
    w1_s[...] = jnp.where(inside & (high >= 4), field, 0)

    def fields(it, carry):
        cols = pl.ds(pl.multiple_of((it // 4) * 128, 128), 128)
        low = pl.multiple_of((it % 4) * 32, 32)
        iota = lax.broadcasted_iota(I32, (32, 128), 0) + low

        def eight(k8, acc):
            acc_0, acc_1 = acc
            rows = pl.ds(pl.multiple_of(k8 * 8, 8), 8)
            lo_8, w0_8, w1_8 = lo_s[rows, cols], w0_s[rows, cols], w1_s[rows, cols]
            for k in range(8):
                same = jnp.broadcast_to(lo_8[k:k + 1, :], (32, 128)) == iota
                acc_0 = acc_0 | jnp.where(same, jnp.broadcast_to(w0_8[k:k + 1, :], (32, 128)), 0)
                acc_1 = acc_1 | jnp.where(same, jnp.broadcast_to(w1_8[k:k + 1, :], (32, 128)), 0)
            return acc_0, acc_1

        zero = jnp.zeros((32, 128), I32)
        acc_0, acc_1 = lax.fori_loop(0, KMAX // 8, eight, (zero, zero))
        u0_t[pl.ds(low, 32), cols] = acc_0
        u1_t[pl.ds(low, 32), cols] = acc_1
        return carry

    lax.fori_loop(0, 16, fields, 0)
    u0[...] = u0_t[...].T
    u1[...] = u1_t[...].T

    loads[4].wait()
    latent = lax.broadcasted_iota(I32, (1, LAT_DEV), 1) + first
    for g in range(GROUPS):
        keep = jnp.where(latent < ends_ref[g], 1.0, 0.0).astype(BF16)
        masked_dec[MAIN * g:MAIN * g + MAIN, :] = dec_v[:MAIN, :] * keep
        at = GROUPS * MAIN + REM * g
        masked_dec[at:at + REM, :] = dec_v[MAIN:, :] * keep

    for j in range(len(PLANE)):
        a1_copy(j).wait_recv()
    total = jnp.zeros((CHUNK, 128), F32)
    for w in range(N_WID):
        total = total + a1_slot[w].astype(F32)
    acts_c[pl.ds(my_rows, CHUNK), :] = jnp.where(
        hit, jnp.maximum(total + my_bias, 0.0), 0.0).astype(BF16)

    def a2_copy(j):
        rows = acts_c.at[pl.ds(my_rows, CHUNK), :]
        return send(rows, rows, a2_send.at[j], a2_recv.at[j], in_plane(j))

    for j in range(len(PLANE)):
        a2_copy(j).start()
        pending.append(a2_copy(j))

    lane_16 = lax.broadcasted_iota(I32, (16, 128), 1)

    def densify(w):
        packed = acts_c[pl.ds(pl.multiple_of(w * CHUNK, CHUNK), CHUNK), :].astype(F32)
        for half in range(2):
            values = pltpu.roll(packed, 1 + KMAX * half, 1)
            values = jnp.where((lane_16 >= 1) & (lane_16 <= KMAX), values, 0.0)
            rows = pl.ds(pl.multiple_of(half * (ROWS // 2) + w * CHUNK, CHUNK), CHUNK)
            words = (u0[rows, :], u1[rows, :])
            for h in range(8):
                slot = (words[h // 4] >> (8 * (h % 4))) & 127
                dens[rows, 128 * h:128 * h + 128] = jnp.take_along_axis(
                    values, slot, 1, mode="promise_in_bounds").astype(BF16)

    densify(wid)
    for group in ARRIVALS:
        for j in group:
            a2_copy(j).wait_recv()
        for j in group:
            densify(plane(j, -1))

    def decode(half, cols):
        rows = pl.ds(pl.multiple_of(half * (ROWS // 2), ROWS // 2), ROWS // 2)
        return lax.dot_general(
            dens[rows, :], masked_dec[cols, :], (((1,), (1,)), ((), ())), preferred_element_type=F32
        ).astype(BF16)

    pieces = [slice(MAIN * g, min(MAIN * g + MAIN, WIDE)) for g in range(GROUPS + 1)]

    def sib_copy(i):
        return send(to_sib.at[:, pieces[i]], from_sib.at[:, pieces[i]], sib_send.at[i], sib_recv.at[i], sibling)

    for i, cols in enumerate(pieces):
        to_sib[:, cols] = decode(1 - core, cols)
        sib_copy(i).start()
        pending.append(sib_copy(i))
    for cols in pieces:
        own[:, cols] = decode(core, cols)
    for i in range(len(pieces)):
        sib_copy(i).wait_recv()

    def chip_sum(offset):
        p = lax.rem(z - offset + N_Z, N_Z)
        rows = pl.ds(pl.multiple_of(p * CHUNK, CHUNK), CHUNK)
        return own[rows, :].astype(F32) + from_sib[rows, :].astype(F32)

    def l1_copy(k):
        return send(l1_src.at[k], l1_slot.at[k], l1_send.at[k], l1_recv.at[k], along_z(LEVEL_1[k][1]))

    def l2_copy(j):
        return send(l2_src.at[j], l2_slot.at[j], l2_send.at[j], l2_recv.at[j], along_z(-CENTRES[j]))

    for k, (offset, _) in enumerate(LEVEL_1):
        l1_src[k] = chip_sum(offset).astype(BF16)
        l1_copy(k).start()
        pending.append(l1_copy(k))
    for i in range(2):
        pl.semaphore_wait(far_ready.at[i], 1)
    for j, centre in enumerate(CENTRES):
        acc = chip_sum(centre)
        for k in members(centre):
            l1_copy(k).wait_recv()
            acc = acc + l1_slot[k].astype(F32)
        l2_src[j] = acc.astype(BF16)
        l2_copy(j).start()
        pending.append(l2_copy(j))
    prefix = chip_sum(0)
    for k in members(0):
        l1_copy(k).wait_recv()
        prefix = prefix + l1_slot[k].astype(F32)
    for j in (2, 3, 0, 1):
        l2_copy(j).wait_recv()
        prefix = prefix + l2_slot[j].astype(F32)

    row_0 = core * (ROWS // 2) + z * CHUNK
    centered = xs[pl.ds(pl.multiple_of(row_0, CHUNK), CHUNK), :]
    err_tail = centered[:, MAIN:] - prefix[:, GROUPS * MAIN:]
    sq_tail = err_tail * err_tail
    row_16 = lax.broadcasted_iota(I32, (16, 128), 0)
    placed = jnp.zeros((16, 128), F32)
    for g in range(GROUPS):
        err = centered[:, :MAIN] - prefix[:, MAIN * g:MAIN * g + MAIN]
        sq = err * err
        sq = sq[:, :128] + sq[:, 128:] + jnp.where(lane_16 // REM == g, sq_tail, 0.0)
        loss = jnp.sum(sq, axis=1, keepdims=True)
        placed = placed + jnp.where(lane_16 == lax.rem(z + g, 8) * 16 + row_16, loss, 0.0)
    partial = jnp.sum(placed, axis=0, keepdims=True)

    def c1_copy(j):
        return send(c1_src, c1_slot.at[wid], c1_send.at[j], c1_recv.at[j], in_plane(j))

    c1_src[...] = partial
    for j in range(len(PLANE)):
        c1_copy(j).start()
        pending.append(c1_copy(j))
    c1_slot[wid] = partial
    for j in range(len(PLANE)):
        c1_copy(j).wait_recv()
    total_loss = c1_slot[0]
    for w in range(1, N_WID):
        total_loss = total_loss + c1_slot[w]
    total_loss = total_loss / (SHARD * N_WID)

    place = core * N_Z + z

    def c2_copy(j):
        dz, dc = COLUMN[j]
        target = (z + dz) % N_Z * 2 + (core + dc) % 2
        return send(c2_src, c2_slot.at[place], c2_send.at[j], c2_recv.at[j], (target, wid))

    c2_src[...] = total_loss
    for j in range(len(COLUMN)):
        c2_copy(j).start()
        pending.append(c2_copy(j))
    c2_slot[place] = total_loss
    for copy in pending:
        copy.wait_send()
    for j in range(len(COLUMN)):
        c2_copy(j).wait_recv()

    lane_8 = lax.broadcasted_iota(I32, (8, 128), 1)
    sub_8 = lax.broadcasted_iota(I32, (8, 128), 0)
    for b in range(ROWS // 128):
        block = jnp.concatenate([c2_slot[8 * b + m] for m in range(8)], axis=0)
        for g in range(GROUPS):
            line = jnp.sum(jnp.where(lane_8 // 16 == (sub_8 + g) % 8, block, 0.0), axis=0, keepdims=True)
            line = jnp.broadcast_to(line, (8, 128))
            if g:
                line = pltpu.roll(line, 128 - 16 * g, 1)
            out_ref[g:g + 1, 128 * b:128 * b + 128] = line[:1, :]


def body(model_acts, picks, group_ends, enc_weight, enc_bias, dec_weight, dec_bias):
    vmem, dma = pltpu.VMEM, pltpu.SemaphoreType.DMA
    half = ROWS // 2
    n_1, n_2 = len(LEVEL_1), len(CENTRES)
    anywhere = pl.BlockSpec(memory_space=pl.ANY)
    losses = pl.pallas_call(
        kernel,
        out_shape=jax.ShapeDtypeStruct((GROUPS, ROWS), F32),
        in_specs=[anywhere, anywhere, pl.BlockSpec(memory_space=pltpu.SMEM)] + [anywhere] * 3
        + [pl.BlockSpec(memory_space=pltpu.VMEM)],
        out_specs=pl.BlockSpec(memory_space=pltpu.VMEM),
        scratch_shapes=[
            vmem((SHARD, ROWS), BF16), vmem((KMAX, ROWS), I32), vmem((SHARD, LAT_DEV), BF16),
            vmem((1, LAT_DEV), F32), vmem((SHARD, LAT_DEV), BF16),
            vmem((ROWS, MAIN + 128), F32), vmem((ROWS, LAT_DEV), F32), vmem((half, 128), I32),
            vmem((KMAX, ROWS), I32), vmem((KMAX, ROWS), I32), vmem((KMAX, ROWS), I32),
            vmem((128, ROWS), I32), vmem((128, ROWS), I32), vmem((ROWS, 128), I32), vmem((ROWS, 128), I32),
            vmem((WIDE, LAT_DEV), BF16),
            vmem((half, 128), BF16), vmem((N_WID, CHUNK, 128), BF16), vmem((half, 128), BF16),
            vmem((ROWS, LAT_DEV), BF16), vmem((half, WIDE), BF16), vmem((half, WIDE), BF16),
            vmem((half, WIDE), BF16),
            vmem((n_1, CHUNK, WIDE), BF16), vmem((n_1, CHUNK, WIDE), BF16),
            vmem((n_2, CHUNK, WIDE), BF16), vmem((n_2, CHUNK, WIDE), BF16),
            vmem((1, 128), F32), vmem((N_WID, 1, 128), F32), vmem((1, 128), F32), vmem((N_LAT, 1, 128), F32),
            dma((5,)), dma((N_WID,)), dma((N_WID,)), dma((N_WID,)), dma((N_WID,)), dma((GROUPS + 1,)), dma((GROUPS + 1,)),
            pltpu.SemaphoreType.REGULAR((2,)), dma((n_1,)), dma((n_1,)), dma((n_2,)), dma((n_2,)),
            dma((N_WID,)), dma((N_WID,)), dma((N_LAT,)), dma((N_LAT,)),
        ],
        compiler_params=pltpu.CompilerParams(
            collective_id=0, has_side_effects=True, vmem_limit_bytes=56 * 2 ** 20),
    )(
        model_acts.T, picks.T, group_ends, enc_weight, enc_bias.reshape(1, -1), dec_weight.T,
        dec_bias,
    )
    return losses.T


def solution(mesh):
    placed = (P(None, "wid"), P(), P(), P("wid", "lat"), P("lat"), P("lat", "wid"), P("wid"))
    return jax.shard_map(body, mesh=mesh, in_specs=placed, out_specs=P(), check_vma=False)
```

time: 71.5 us -> 62.4 us (0.87)
  local copies, waits for them, and re-layouts: 5.93 us -> 1.3 us
  Pallas kernels: 65.3 us -> 60.9 us
    unnamed x15 -> x1, local copies, waits for them, and re-layouts: 5.93 us -> 1.3 us
    pallas_call x1, Pallas kernels: 65.3 us -> 60.9 us  [body(): pl.pallas_call(kernel, out_shape=jax.ShapeDtypeStruct((GROUPS, ROWS), F32...]
where the time goes in v2:
time: 62.4 us; the launch traced here: 62.2 us
  Pallas kernels  60.9 us (98%)
  local copies, waits for them, and re-layouts  1.3 us (2%)
    pallas_call x1, Pallas kernels, body(): pl.pallas_call(kernel, out_shape=jax.ShapeDtypeStruct((GROUPS, ROWS), F32...  60.9 us
    unnamed x1, local copies, waits for them, and re-layouts  1.3 us

profile of v2, /device:TPU:1, one launch (start us, length us, event | category | flops | bytes accessed | tf_op | source)
XLA Modules:
  0.0 62.2 jit_solution(2016172205793642280)
XLA Ops:
  0.0 60.9 %shard_map.73 = f32[4,512]{1,0:T(4,128)} custom-call(bf16[288,512]{1,0:T(8,128)(2,1)} %bitcast.6, s32[64,512]{1,0:T(8,128)} %bitcast.7, s32[4]{0:T(128)} %ends_ref.1, bf16[288,1024]{1,0:T(8,128)(2,1)} %encw_hbm.1, f32[1,1024]{1,0:T(1,128)} %bitcast.9, bf16[288,1024]{1,0:T(8,128)(2,1)} %bitcast.5, f32[288]{0:T(512)} %decb_v.1), custom_call_target="tpu_custom_call" | custom-call | tf_op jit(solution)/shard_map/pallas_call | solution.py:354
  60.9 1.3 %copy.9 = f32[512,4]{0,1:T(4,128)} copy(f32[512,4]{0,1:T(4,128)} %bitcast.8) | data formatting | bytes 16384

commit v3 on v2

--- a/solution.py
+++ b/solution.py
@@ -10,7 +10,7 @@
 SHARD, MAIN = 288, 256
 REM = SHARD - MAIN
 LAT_DEV = 1024
-EXTRACT = 32
+EXTRACT = 64
 N_LAT, N_WID, N_Z = 32, 16, 16
 CHUNK = 16
 WIDE = GROUPS * SHARD
@@ -20,7 +20,9 @@
     (2, 1), (4, -1), (-4, 1), (-2, -1),
     (1, -1), (-1, 1),
 )
+LEVEL_1 = (LEVEL_1, LEVEL_1[:4] + ((-8, 2),) + LEVEL_1[5:])
 CENTRES = (6, -6, 3, -3)
+PIECES = (slice(0, 768), slice(768, WIDE))
 Z_PEERS = (3, -3, 2, -2, 1, -1)
 
 
@@ -33,11 +35,11 @@
     key=lambda d: -(ring(d[0], 4) + ring(d[1], 4)))
 COLUMN = sorted(
     ((dz, dc) for dz in range(N_Z) for dc in range(2) if dz or dc), key=lambda d: -ring(d[0], N_Z))
-ARRIVALS = (range(14, 4, -1), range(4, -1, -1))
-
-
-def members(centre):
-    return [k for k, (offset, dz) in enumerate(LEVEL_1) if offset + dz == centre]
+ARRIVALS = (range(14, 10, -1), range(10, 4, -1), range(4, -1, -1))
+
+
+def members(i, centre):
+    return [k for k, (offset, dz) in enumerate(LEVEL_1[i % 2]) if offset + dz == centre]
 
 
 def kernel(
@@ -47,7 +49,7 @@
     a1_src, a1_slot, acts_c, dens, to_sib, own, from_sib,
     l1_src, l1_slot, l2_src, l2_slot, c1_src, c1_slot, c2_src, c2_slot,
     in_sem, a1_send, a1_recv, a2_send, a2_recv, sib_send, sib_recv,
-    far_ready, l1_send, l1_recv, l2_send, l2_recv, c1_send, c1_recv, c2_send, c2_recv,
+    l1_send, l1_recv, l2_send, l2_recv, c1_send, c1_recv, c2_send, c2_recv,
 ):
     lat = lax.axis_index("lat")
     wid = lax.axis_index("wid")
@@ -79,6 +81,8 @@
              (encb_hbm, encb_v), (dec_hbm, dec_v))
         )
     ]
+    for load in loads:
+        load.start()
     barrier = pltpu.get_barrier_semaphore()
 
     def greet(device):
@@ -89,12 +93,10 @@
     for j in range(len(PLANE)):
         greet(in_plane(j))
     greet(sibling)
-    for load in loads:
-        load.start()
     pending = []
 
-    loads[0].wait()
-    loads[1].wait()
+    for load in loads[:4]:
+        load.wait()
     x_t = x_v[...].astype(F32)
     tail = x_t[MAIN:, :]
     lanes_1 = lax.broadcasted_iota(I32, (1, 128), 1)
@@ -109,8 +111,6 @@
         xs[:, :SHARD].astype(BF16), encw_v[...], preferred_element_type=F32
     )
 
-    loads[2].wait()
-    loads[3].wait()
     local = picks_v[...] - first
     ids[...] = jnp.concatenate([local[:, :ROWS // 2], local[:, ROWS // 2:]], axis=0).T
 
@@ -144,9 +144,6 @@
     for j in range(len(PLANE)):
         a1_copy(j).start()
         pending.append(a1_copy(j))
-    for i, step in enumerate((3, -3)):
-        pl.semaphore_signal(
-            far_ready.at[i], inc=1, device_id=along_z(step), device_id_type=pl.DeviceIdType.MESH)
     my_rows = pl.multiple_of(wid * CHUNK, CHUNK)
     a1_slot[wid] = a1_src[pl.ds(my_rows, CHUNK), :]
 
@@ -241,53 +238,63 @@
             dens[rows, :], masked_dec[cols, :], (((1,), (1,)), ((), ())), preferred_element_type=F32
         ).astype(BF16)
 
-    pieces = [slice(MAIN * g, min(MAIN * g + MAIN, WIDE)) for g in range(GROUPS + 1)]
-
     def sib_copy(i):
-        return send(to_sib.at[:, pieces[i]], from_sib.at[:, pieces[i]], sib_send.at[i], sib_recv.at[i], sibling)
-
-    for i, cols in enumerate(pieces):
+        cols = PIECES[i]
+        return send(to_sib.at[:, cols], from_sib.at[:, cols], sib_send.at[i], sib_recv.at[i], sibling)
+
+    def chip_sum(i, offset):
+        p = lax.rem(z - offset + N_Z, N_Z)
+        rows = pl.ds(pl.multiple_of(p * CHUNK, CHUNK), CHUNK)
+        return own[rows, PIECES[i]].astype(F32) + from_sib[rows, PIECES[i]].astype(F32)
+
+    def l1_copy(i, k):
+        return send(l1_src.at[k, :, PIECES[i]], l1_slot.at[k, :, PIECES[i]], l1_send.at[i, k], l1_recv.at[i, k],
+                    along_z(LEVEL_1[i % 2][k][1]))
+
+    def l2_copy(i, j):
+        step = -3 if CENTRES[j] > 0 else 3
+        return send(l2_src.at[j, :, PIECES[i]], l2_slot.at[j, :, PIECES[i]], l2_send.at[i, j], l2_recv.at[i, j],
+                    along_z(step))
+
+    def l1_sum(i, centre):
+        acc = chip_sum(i, centre)
+        for k in members(i, centre):
+            l1_copy(i, k).wait_recv()
+            acc = acc + l1_slot[k, :, PIECES[i]].astype(F32)
+        return acc
+
+    for i, cols in enumerate(PIECES):
         to_sib[:, cols] = decode(1 - core, cols)
         sib_copy(i).start()
         pending.append(sib_copy(i))
-    for cols in pieces:
+    for i, cols in enumerate(PIECES):
         own[:, cols] = decode(core, cols)
-    for i in range(len(pieces)):
         sib_copy(i).wait_recv()
-
-    def chip_sum(offset):
-        p = lax.rem(z - offset + N_Z, N_Z)
-        rows = pl.ds(pl.multiple_of(p * CHUNK, CHUNK), CHUNK)
-        return own[rows, :].astype(F32) + from_sib[rows, :].astype(F32)
-
-    def l1_copy(k):
-        return send(l1_src.at[k], l1_slot.at[k], l1_send.at[k], l1_recv.at[k], along_z(LEVEL_1[k][1]))
-
-    def l2_copy(j):
-        return send(l2_src.at[j], l2_slot.at[j], l2_send.at[j], l2_recv.at[j], along_z(-CENTRES[j]))
-
-    for k, (offset, _) in enumerate(LEVEL_1):
-        l1_src[k] = chip_sum(offset).astype(BF16)
-        l1_copy(k).start()
-        pending.append(l1_copy(k))
-    for i in range(2):
-        pl.semaphore_wait(far_ready.at[i], 1)
-    for j, centre in enumerate(CENTRES):
-        acc = chip_sum(centre)
-        for k in members(centre):
-            l1_copy(k).wait_recv()
-            acc = acc + l1_slot[k].astype(F32)
-        l2_src[j] = acc.astype(BF16)
-        l2_copy(j).start()
-        pending.append(l2_copy(j))
-    prefix = chip_sum(0)
-    for k in members(0):
-        l1_copy(k).wait_recv()
-        prefix = prefix + l1_slot[k].astype(F32)
-    for j in (2, 3, 0, 1):
-        l2_copy(j).wait_recv()
-        prefix = prefix + l2_slot[j].astype(F32)
-
+        for k, (offset, _) in enumerate(LEVEL_1[i % 2]):
+            l1_src[k, :, cols] = chip_sum(i, offset).astype(BF16)
+            l1_copy(i, k).start()
+            pending.append(l1_copy(i, k))
+
+    for i, cols in enumerate(PIECES):
+        for j in (0, 1):
+            l2_src[j, :, cols] = l1_sum(i, CENTRES[j]).astype(BF16)
+            l2_copy(i, j).start()
+            pending.append(l2_copy(i, j))
+    for i, cols in enumerate(PIECES):
+        for j in (2, 3):
+            acc = l1_sum(i, CENTRES[j])
+            l2_copy(i, j - 2).wait_recv()
+            l2_src[j, :, cols] = (acc + l2_slot[j - 2, :, cols].astype(F32)).astype(BF16)
+            l2_copy(i, j).start()
+            pending.append(l2_copy(i, j))
+    parts = []
+    for i, cols in enumerate(PIECES):
+        acc = l1_sum(i, 0)
+        for j in (2, 3):
+            l2_copy(i, j).wait_recv()
+            acc = acc + l2_slot[j, :, cols].astype(F32)
+        parts.append(acc)
+    prefix = jnp.concatenate(parts, axis=1)
     row_0 = core * (ROWS // 2) + z * CHUNK
     centered = xs[pl.ds(pl.multiple_of(row_0, CHUNK), CHUNK), :]
     err_tail = centered[:, MAIN:] - prefix[:, GROUPS * MAIN:]
@@ -349,7 +356,7 @@
 def body(model_acts, picks, group_ends, enc_weight, enc_bias, dec_weight, dec_bias):
     vmem, dma = pltpu.VMEM, pltpu.SemaphoreType.DMA
     half = ROWS // 2
-    n_1, n_2 = len(LEVEL_1), len(CENTRES)
+    n_1, n_2, n_p = len(LEVEL_1[0]), len(CENTRES), len(PIECES)
     anywhere = pl.BlockSpec(memory_space=pl.ANY)
     losses = pl.pallas_call(
         kernel,
@@ -370,8 +377,8 @@
             vmem((n_1, CHUNK, WIDE), BF16), vmem((n_1, CHUNK, WIDE), BF16),
             vmem((n_2, CHUNK, WIDE), BF16), vmem((n_2, CHUNK, WIDE), BF16),
             vmem((1, 128), F32), vmem((N_WID, 1, 128), F32), vmem((1, 128), F32), vmem((N_LAT, 1, 128), F32),
-            dma((5,)), dma((N_WID,)), dma((N_WID,)), dma((N_WID,)), dma((N_WID,)), dma((GROUPS + 1,)), dma((GROUPS + 1,)),
-            pltpu.SemaphoreType.REGULAR((2,)), dma((n_1,)), dma((n_1,)), dma((n_2,)), dma((n_2,)),
+            dma((5,)), dma((N_WID,)), dma((N_WID,)), dma((N_WID,)), dma((N_WID,)), dma((n_p,)), dma((n_p,)),
+            dma((n_p, n_1)), dma((n_p, n_1)), dma((n_p, n_2)), dma((n_p, n_2)),
             dma((N_WID,)), dma((N_WID,)), dma((N_LAT,)), dma((N_LAT,)),
         ],
         compiler_params=pltpu.CompilerParams(

time: 62.4 us -> 59.4 us (0.952)
  Pallas kernels: 60.9 us -> 57.9 us
    pallas_call x1, Pallas kernels: 60.9 us -> 57.9 us  [body(): pl.pallas_call(kernel, out_shape=jax.ShapeDtypeStruct((GROUPS, ROWS), F32...]
where the time goes in v3:
time: 59.4 us; the launch traced here: 59.2 us
  Pallas kernels  57.9 us (97%)
  local copies, waits for them, and re-layouts  1.3 us (2%)
    pallas_call x1, Pallas kernels, body(): pl.pallas_call(kernel, out_shape=jax.ShapeDtypeStruct((GROUPS, ROWS), F32...  57.9 us
    unnamed x1, local copies, waits for them, and re-layouts  1.3 us

profile of v3, /device:TPU:1, one launch (start us, length us, event | category | flops | bytes accessed | tf_op | source)
XLA Modules:
  0.0 59.2 jit_solution(877216925975925963)
XLA Ops:
  0.0 57.9 %shard_map.73 = f32[4,512]{1,0:T(4,128)} custom-call(bf16[288,512]{1,0:T(8,128)(2,1)} %bitcast.6, s32[64,512]{1,0:T(8,128)} %bitcast.7, s32[4]{0:T(128)} %ends_ref.1, bf16[288,1024]{1,0:T(8,128)(2,1)} %encw_hbm.1, f32[1,1024]{1,0:T(1,128)} %bitcast.9, bf16[288,1024]{1,0:T(8,128)(2,1)} %bitcast.5, f32[288]{0:T(512)} %decb_v.1), custom_call_target="tpu_custom_call" | custom-call | tf_op jit(solution)/shard_map/pallas_call | solution.py:361
  57.9 1.3 %copy.9 = f32[512,4]{0,1:T(4,128)} copy(f32[512,4]{0,1:T(4,128)} %bitcast.8) | data formatting | bytes 16384

commit v4 on v3

--- a/solution.py
+++ b/solution.py
@@ -22,7 +22,7 @@
 )
 LEVEL_1 = (LEVEL_1, LEVEL_1[:4] + ((-8, 2),) + LEVEL_1[5:])
 CENTRES = (6, -6, 3, -3)
-PIECES = (slice(0, 768), slice(768, WIDE))
+PIECES = (slice(0, 384), slice(384, WIDE))
 Z_PEERS = (3, -3, 2, -2, 1, -1)
 
 
@@ -360,7 +360,7 @@
     anywhere = pl.BlockSpec(memory_space=pl.ANY)
     losses = pl.pallas_call(
         kernel,
-        out_shape=jax.ShapeDtypeStruct((GROUPS, ROWS), F32),
+        out_shape=pltpu.VMEM((GROUPS, ROWS), F32),
         in_specs=[anywhere, anywhere, pl.BlockSpec(memory_space=pltpu.SMEM)] + [anywhere] * 3
         + [pl.BlockSpec(memory_space=pltpu.VMEM)],
         out_specs=pl.BlockSpec(memory_space=pltpu.VMEM),

time: 59.4 us -> 57.1 us (0.961)
  Pallas kernels: 57.9 us -> 56.4 us
  local copies, waits for them, and re-layouts: 1.3 us -> 0.6 us
    pallas_call x1, Pallas kernels: 57.9 us -> 56.4 us  [body(): pl.pallas_call(kernel, out_shape=pltpu.VMEM((GROUPS, ROWS), F32), in_spec...]
    unnamed x1, local copies, waits for them, and re-layouts: 1.3 us -> 0.6 us
where the time goes in v4:
time: 57.1 us; the launch traced here: 57 us
  Pallas kernels  56.4 us (99%)
  local copies, waits for them, and re-layouts  0.6 us (1%)
    pallas_call x1, Pallas kernels, body(): pl.pallas_call(kernel, out_shape=pltpu.VMEM((GROUPS, ROWS), F32), in_spec...  56.4 us

profile of v4, /device:TPU:1, one launch (start us, length us, event | category | flops | bytes accessed | tf_op | source)
XLA Modules:
  0.0 57.0 jit_solution(5413367147671848955)
XLA Ops:
  0.0 56.4 %shard_map.73 = f32[4,512]{1,0:T(4,128)S(1)} custom-call(bf16[288,512]{1,0:T(8,128)(2,1)} %bitcast.7, s32[64,512]{1,0:T(8,128)} %bitcast.8, s32[4]{0:T(128)} %ends_ref.1, bf16[288,1024]{1,0:T(8,128)(2,1)} %encw_hbm.1, f32[1,1024]{1,0:T(1,128)} %bitcast.9, bf16[288,1024]{1,0:T(8,128)(2,1)} %bitcast.6, f32[288]{0:T(512)} %decb_v.1), custom_call_target="tpu_custom_call" | custom-call | tf_op jit(solution)/shard_map/pallas_call | solution.py:361
  56.4 0.6 %copy.9 = f32[512,4]{0,1:T(4,128)} copy(f32[512,4]{0,1:T(4,128)S(1)} %bitcast.5) | data formatting | bytes 16384

commit v5 on v4

--- a/solution.py
+++ b/solution.py
@@ -22,7 +22,7 @@
 )
 LEVEL_1 = (LEVEL_1, LEVEL_1[:4] + ((-8, 2),) + LEVEL_1[5:])
 CENTRES = (6, -6, 3, -3)
-PIECES = (slice(0, 384), slice(384, WIDE))
+PIECES = (slice(0, 256), slice(256, WIDE))
 Z_PEERS = (3, -3, 2, -2, 1, -1)
 
 

time: 57.1 us -> 57.5 us (level)
  no operation moved by 1% of the time
where the time goes in v5:
time: 57.5 us; the launch traced here: 57.3 us
  Pallas kernels  56.7 us (99%)
  local copies, waits for them, and re-layouts  0.6 us (1%)
    pallas_call x1, Pallas kernels, body(): pl.pallas_call(kernel, out_shape=pltpu.VMEM((GROUPS, ROWS), F32), in_spec...  56.7 us

profile of v5, /device:TPU:1, one launch (start us, length us, event | category | flops | bytes accessed | tf_op | source)
XLA Modules:
  0.0 57.3 jit_solution(7829929815983552735)
XLA Ops:
  0.0 56.7 %shard_map.73 = f32[4,512]{1,0:T(4,128)S(1)} custom-call(bf16[288,512]{1,0:T(8,128)(2,1)} %bitcast.7, s32[64,512]{1,0:T(8,128)} %bitcast.8, s32[4]{0:T(128)} %ends_ref.1, bf16[288,1024]{1,0:T(8,128)(2,1)} %encw_hbm.1, f32[1,1024]{1,0:T(1,128)} %bitcast.9, bf16[288,1024]{1,0:T(8,128)(2,1)} %bitcast.6, f32[288]{0:T(512)} %decb_v.1), custom_call_target="tpu_custom_call" | custom-call | tf_op jit(solution)/shard_map/pallas_call | solution.py:361
  56.7 0.6 %copy.9 = f32[512,4]{0,1:T(4,128)} copy(f32[512,4]{0,1:T(4,128)S(1)} %bitcast.5) | data formatting | bytes 16384
